TPU v7x, 32 devices: a whole 2x2x4 slice. The times are simulated.
32 devices in a mesh: groups: 2 (over y), ctx: 4 (over z), head: 2 (over x), user: 2 (over core).
Axes of the slice: x: 2, y: 2, z: 4, core: 2. Of those that a mesh axis runs over, the one named last changes fastest.
Arguments:
- projected: bfloat16 [4, 2048, 8, 4, 128], P(('groups', 'user'), 'ctx', 'head'), parts along dimension 0, may hold values from -6 to 6
- upstream: bfloat16 [4, 2048, 8, 128], P(('groups', 'user'), 'ctx', 'head'), parts along dimension 0, may hold values from -6 to 6
- ips_weight: float32 [4, 2048], P(('groups', 'user')), parts along dimension 0, may hold values from 0.2 to 5
- item_ids: int32 [4, 2048], P(('groups', 'user')), parts along dimension 0, may hold values from 0 to 999
- session_ids: int32 [4, 2048], P(('groups', 'user')), parts along dimension 0, may hold values from 0 to 7, never falling along the last dimension, each value on 1 to 1024 neighbouring positions
- session_blocks: int32 [4, 4, 3], P(('groups', 'user')), parts along dimension 0, may hold values from -1 to 1, as said below
Outputs:
- mixed: bfloat16 [4, 2048, 8, 128], P(('groups', 'user'), 'ctx', 'head'), parts along dimension 0
- proj_grad: bfloat16 [4, 2048, 8, 4, 128], P(('groups', 'user'), 'ctx', 'head'), parts along dimension 0
There are 2 independent parts, one for each index of `groups`. A program takes and returns all parts, laid end to end along the dimension named above; each array names one. Nothing has to cross between parts.
Inputs may be any that keep to these rules, and one draw needn't show every extreme that they name: `session_blocks`: row b lists, in ascending order, distinct blocks below b, and -1 in the remaining slots; row 3 always lists block 1 and never block 2, and row 1 never lists block 0.
All inputs are finite; a program needn't handle non-finite values.
Results may differ from a plain program's by a relative error of at most 0.0056.
Values may be sent and summed in bfloat16 or wider, within the bound.
A program may use at most 128 MiB of HBM per device.

v0:
```python
import jax
import jax.numpy as jnp
from jax import lax
from jax.sharding import PartitionSpec as P

BLOCK = 512


def shifted_2(block, axis, distance):
    devices = range(lax.axis_size(axis))
    route = [(i - distance, i) for i in devices if i - distance in devices]
    return lax.ppermute(block, axis, route)


def pair_scores(queries, keys):
    scale = queries.shape[-1] ** (-0.5)
    return jnp.einsum("ahd,chd->hac", queries, keys, preferred_element_type=jnp.float32) * scale


def attend(queries, keys, values, visible):
    scores = pair_scores(queries, keys)
    probs = jnp.where(visible[None], jax.nn.silu(scores), 0.0).astype(jnp.bfloat16)
    return jnp.einsum("hac,chd->ahd", probs, values, preferred_element_type=jnp.float32)


def attend_back(queries, grad_rows, keys, values, visible):
    scale = queries.shape[-1] ** (-0.5)
    scores = pair_scores(queries, keys)
    sigma = jax.nn.sigmoid(scores)
    probs = jnp.where(visible[None], jax.nn.silu(scores), 0.0).astype(jnp.bfloat16)
    slope = sigma * (1.0 + scores * (1.0 - sigma))
    dprod = jnp.einsum("ahd,chd->hac", grad_rows, values, preferred_element_type=jnp.float32)
    edges = jnp.where(visible[None], dprod * slope, 0.0).astype(jnp.bfloat16)
    grad_q = jnp.einsum("hac,chd->ahd", edges, keys, preferred_element_type=jnp.float32) * scale
    grad_k = jnp.einsum("hac,ahd->chd", edges, queries, preferred_element_type=jnp.float32) * scale
    grad_v = jnp.einsum("hac,ahd->chd", probs, grad_rows, preferred_element_type=jnp.float32)
    return (grad_q, grad_k, grad_v)


def shards(projected, upstream, ips_weight, item_ids, session_ids, session_blocks):
    rows = projected[0]
    count = rows.shape[0]
    heads = rows.shape[1]
    width = rows.shape[3]
    block = BLOCK
    local_blocks = count // block
    ctx_rank = lax.axis_index("ctx")
    first = ctx_rank * local_blocks
    sessions = session_ids[0]
    lists = session_blocks[0]
    gates = rows[:, :, 0]
    queries = rows[:, :, 1].reshape(local_blocks, block, heads, width)
    pairs = rows[:, :, 2:4]
    pair_blocks = pairs.reshape(local_blocks, block, heads, 2, width)
    inner = jnp.arange(block)
    below = inner[None, :] <= inner[:, None]
    everything = jnp.ones((block, block), bool)

    def session_slice(index):
        return lax.dynamic_slice_in_dim(sessions, jnp.maximum(index, 0) * block, block)

    list_rows = []
    local = 0
    glob = first + local
    here = session_slice(glob)
    there = session_slice(glob - 1)
    list_row = lax.dynamic_index_in_dim(lists, glob, 0, keepdims=False)
    prev_listed = jnp.any(list_row == glob - 1)
    own_masks = [below & (here[:, None] == here[None, :])]
    prev_masks = [
        jnp.logical_not(below)
        & (here[:, None] == there[None, :])
        & (glob > 0)
        & jnp.logical_not(prev_listed)
    ]
    list_rows.append(list_row)
    previous = shifted_2(pair_blocks[local_blocks - 1], "ctx", 1)
    prior = [previous] + [pair_blocks[local] for local in range(local_blocks - 1)]
    local = 0
    current = pair_blocks[local]
    total = attend(queries[local], current[:, :, 0], current[:, :, 1], own_masks[local])
    total = total + attend(
        queries[local], prior[local][:, :, 0], prior[local][:, :, 1], prev_masks[local]
    )
    totals = [total]
    piece_blocks = lax.all_gather(pairs, "ctx", axis=0, tiled=True).reshape(
        -1, block, heads, 2, width
    )

    def visit(index, acc):
        chosen = lax.dynamic_index_in_dim(piece_blocks, index, 0, keepdims=False)
        local = 0
        hit = jnp.any(list_rows[local] == index)
        updated = [
            lax.cond(
                hit,
                lambda value, local=local: value
                + attend(queries[local], chosen[:, :, 0], chosen[:, :, 1], everything),
                lambda value: value,
                acc[local],
            )
        ]
        return tuple(updated)

    summed = lax.fori_loop(0, piece_blocks.shape[0], visit, tuple(totals))
    attended = summed[0]
    centre = jnp.mean(attended, -1, keepdims=True)
    shifted = attended - centre
    inv_std = lax.rsqrt(jnp.mean(shifted * shifted, -1, keepdims=True) + 1e-05)
    normed = shifted * inv_std
    gates_f = gates.astype(jnp.float32)
    mixed = (normed * gates_f).astype(jnp.bfloat16)
    weights_row = ips_weight[0]
    items = item_ids[0]
    fresh = jnp.concatenate(
        [(items[1:] != items[:-1]).astype(jnp.float32), jnp.zeros((1,), jnp.float32)]
    )
    scaled = weights_row * fresh * weights_row.shape[0] / jnp.sum(weights_row)
    local_scale = lax.dynamic_slice_in_dim(scaled, ctx_rank * count, count)
    grad_mixed = local_scale[:, None, None] * upstream[0].astype(jnp.float32)
    grad_gates = (grad_mixed * normed).astype(jnp.bfloat16)
    grad_normed = grad_mixed * gates_f
    grad_att = inv_std * (
        grad_normed
        - jnp.mean(grad_normed, -1, keepdims=True)
        - normed * jnp.mean(grad_normed * normed, -1, keepdims=True)
    )
    grad_flat = grad_att.astype(jnp.bfloat16)
    grad_rows = grad_flat.reshape(local_blocks, block, heads, width)
    grad_q = []
    grad_kv = []
    local = 0
    current = pair_blocks[local]
    own_q, own_k, own_v = attend_back(
        queries[local], grad_rows[local], current[:, :, 0], current[:, :, 1], own_masks[local]
    )
    near_q, near_k, near_v = attend_back(
        queries[local],
        grad_rows[local],
        prior[local][:, :, 0],
        prior[local][:, :, 1],
        prev_masks[local],
    )
    grad_q.append(own_q + near_q)
    grad_kv.append(jnp.stack([own_k, own_v], 2))
    backward_prev = jnp.stack([near_k, near_v], 2)
    incoming = shifted_2(backward_prev.astype(jnp.bfloat16), "ctx", -1).astype(jnp.float32)
    grad_kv[local_blocks - 1] = grad_kv[local_blocks - 1] + incoming
    pulled = jnp.stack([rows[:, :, 1], grad_flat], 2)
    piece_pairs = lax.all_gather(pairs, "ctx", axis=0, tiled=True).reshape(
        -1, block, heads, 2, width
    )
    piece_pulled = lax.all_gather(pulled, "ctx", axis=0, tiled=True).reshape(
        -1, block, heads, 2, width
    )

    def visit(index, acc):
        sums, owned = acc
        chosen = lax.dynamic_index_in_dim(piece_pairs, index, 0, keepdims=False)
        asked = lax.dynamic_index_in_dim(piece_pulled, index, 0, keepdims=False)
        target_list = lax.dynamic_index_in_dim(lists, index, 0, keepdims=False)
        local = 0
        hit = jnp.any(list_rows[local] == index)
        new_sums = [
            lax.cond(
                hit,
                lambda value, local=local: value
                + attend_back(
                    queries[local], grad_rows[local], chosen[:, :, 0], chosen[:, :, 1], everything
                )[0],
                lambda value: value,
                sums[local],
            )
        ]
        mine = jnp.any(target_list == first + local)

        def owner_add(value, local=local):
            part_q, part_k, part_v = attend_back(
                asked[:, :, 0],
                asked[:, :, 1],
                pair_blocks[local][:, :, 0],
                pair_blocks[local][:, :, 1],
                everything,
            )
            return value + jnp.stack([part_k, part_v], 2)

        new_owned = [lax.cond(mine, owner_add, lambda value: value, owned[local])]
        return (tuple(new_sums), tuple(new_owned))

    sums, owned = lax.fori_loop(0, piece_pairs.shape[0], visit, (tuple(grad_q), tuple(grad_kv)))
    grad_q = list(sums)
    grad_kv = list(owned)
    grad_q_all = grad_q[0].astype(jnp.bfloat16)
    grad_kv_all = grad_kv[0].astype(jnp.bfloat16)
    result = jnp.concatenate([grad_gates[:, :, None], grad_q_all[:, :, None], grad_kv_all], 2)
    return (mixed[None], result[None])


def solution(mesh):
    placed = (
        P(("groups", "user"), "ctx", "head", None, None),
        P(("groups", "user"), "ctx", "head", None),
        P(("groups", "user"), None),
        P(("groups", "user"), None),
        P(("groups", "user"), None),
        P(("groups", "user"), None, None),
    )
    return jax.shard_map(
        shards,
        mesh=mesh,
        in_specs=placed,
        out_specs=(
            P(("groups", "user"), "ctx", "head", None),
            P(("groups", "user"), "ctx", "head", None, None),
        ),
        check_vma=False,
    )
```

profile of v0, /device:TPU:12, one launch (start us, length us, event | category | flops | bytes accessed | tf_op | source)
XLA Modules:
  0.0 296.6 jit_solution(7141404065452275830)
XLA Ops:
  7.3 2.1 copy.71
  10.6 3.5 %collective-permute-start = (bf16[512,4,2,128]{3,0,1,2:T(8,128)(2,1)}, bf16[512,4,2,128]{3,0,1,2:T(8,128)(2,1)S(1)}, u32[]{:S(2)}, u32[]{:S(2)}) collective-permute-start(bf16[512,4,2,128]{3,0,1,2:T(8,128)(2,1)} %slice.88), channel_id=1, source_target_pairs={{0,4},{4,8},{8,12},{1,5},{5,9},{9,13},{2,6},{6,10},{10,14},{3,7},{... | collective-permute-start | bytes 3145736 | tf_op jit(solution)/shard_map/ppermute | solution.py:12
  18.6 3.6 %select_convert_fusion.3 = (bf16[4,512,512]{2,1,0:T(8,128)(2,1)S(1)}, f32[4,512,512]{2,1,0:T(8,128)}) fusion(pred[512,512]{1,0:T(8,128)(4,1)S(1)} %get-tuple-element.484, bf16[512,4,4,128]{3,0,1,2:T(8,128)(2,1)S(1)} %bitcast.218), kind=kOutput, calls=%fused_computation.64 | convolution fusion | flops 275775488 | bytes 7602176 | tf_op jit(solution)/shard_map/ahd,chd->hac/dot_general | solution.py:17
  22.9 47.2 %collective-permute-done = bf16[512,4,2,128]{3,0,1,2:T(8,128)(2,1)S(1)} collective-permute-done((bf16[512,4,2,128]{3,0,1,2:T(8,128)(2,1)}, bf16[512,4,2,128]{3,0,1,2:T(8,128)(2,1)S(1)}, u32[]{:S(2)}, u32[]{:S(2)}) %collective-permute-start) | collective-permute-done | bytes 1048608 | tf_op jit(solution)/shard_map/ppermute | solution.py:12
  70.1 3.6 %select_convert_fusion.2 = (bf16[4,512,512]{2,1,0:T(8,128)(2,1)S(1)}, f32[4,512,512]{2,1,0:T(8,128)}) fusion(pred[512,512]{1,0:T(8,128)(4,1)S(1)} %get-tuple-element.483, bf16[512,4,2,128]{3,0,1,2:T(8,128)(2,1)S(1)} %collective-permute-done, bf16[512,4,4,128]{3,0,1,2:T(8,128)(2,1)S(1)} %bitcast.220), kind=kOutput, calls=%fused_computation.62 | convolution fusion | flops 275775488 | bytes 7602176 | tf_op jit(solution)/shard_map/ahd,chd->hac/dot_general | solution.py:17
  75.7 30.0 %all-gather.3.cloned.1.call-done = bf16[2048,4,2,128]{3,0,1,2:T(8,128)(2,1)} async-done(((bf16[512,4,2,128]{3,0,1,2:T(8,128)(2,1)}), bf16[2048,4,2,128]{3,0,1,2:T(8,128)(2,1)}) %all-gather.3.cloned.1.call-update) | async-done | bytes 4194320 | tf_op jit(solution)/shard_map/all_gather | solution.py:86
  105.8 4.6 %copy.34 = bf16[4,512,4,2,128]{4,1,2,3,0:T(8,128)(2,1)} copy(bf16[4,512,4,2,128]{4,1,0,2,3:T(8,128)(2,1)} %bitcast.228) | data formatting | bytes 8388608 | tf_op jit(solution)/shard_map/while | solution.py:105
  110.3 5.4 %while.37 = (s32[]{:T(128)}, f32[512,4,128]{2,0,1:T(8,128)S(1)}, s32[3]{0:T(128)S(1)}, bf16[4,512,4,2,128]{4,1,2,3,0:T(8,128)(2,1)}, bf16[512,4,1,128]{3,0,1,2:T(8,128)(2,1)}, /*index=5*/s32[]{:T(128)}) while((s32[]{:T(128)}, f32[512,4,128]{2,0,1:T(8,128)S(1)}, s32[3]{0:T(128)S(1)}, bf16[4,512,4,2,128]{4,1,2,3,0:T(8,128)(2,1)}, ...), condition=%wide.region_5.6_spmd, body=%wide.region_1.5_spmd.sunk | while | flops 543424512 | bytes 5767345 | solution.py:105
  116.8 3.1 %fusion.59 = (f32[512,4]{0,1:T(4,128)S(1)}, f32[512,4]{0,1:T(4,128)S(1)}, bf16[512,4,1,128]{3,0,1,2:T(8,128)(2,1)}) fusion(f32[512]{0:T(512)S(1)} %fusion.71, bf16[512,4,4,128]{3,0,1,2:T(8,128)(2,1)} %bitcast.221, bf16[1,512,4,128]{3,2,1,0:T(4,128)(2,1)} %param.17, f32[512,4]{0,1:T(4,128)S(1)} %add_rsqrt_fusion, f32[512,4,128]{2,0,1:T(8,128)S(1)} %get-tuple-element.405, ...), kind=kLoop, calls=%fused_computation.101 | loop fusion | flops 2879488 | bytes 2656256 | tf_op jit(solution)/shard_map/reduce_sum | solution.py:125
  120.0 3.0 %multiply_convert_fusion.5 = (bf16[512,4,128]{2,0,1:T(8,128)(2,1)S(1)}, bf16[1,512,4,128]{3,1,2,0:T(8,128)(2,1)}) fusion(f32[512,4,128]{2,0,1:T(8,128)S(1)} %get-tuple-element.405, f32[512,4]{0,1:T(4,128)S(1)} %get-tuple-element.489, f32[512,4]{0,1:T(4,128)S(1)} %get-tuple-element.490, f32[512]{0:T(512)S(1)} %fusion.71, f32[512,4]{0,1:T(4,128)S(1)} %add_rsqrt_fusion, ...), kind=kLoop, calls=%fused_computation.91 | loop fusion | flops 3407872 | bytes 3180544 | tf_op jit(solution)/shard_map/convert_element_type | solution.py:128
  123.7 2.2 pad_maximum_fusion.1
  126.0 2.4 copy.44
  128.5 2.2 copy.49
  130.7 1.8 copy.47
  133.5 3.8 %select_convert_fusion = bf16[4,512,512]{2,1,0:T(8,128)(2,1)S(1)} fusion(f32[4,512,512]{2,1,0:T(8,128)} %get-tuple-element.488, bf16[512,4,128]{2,0,1:T(8,128)(2,1)S(1)} %copy-done.4, pred[512,512]{1,0:T(8,128)(4,1)S(1)} %copy-done.14, bf16[512,4,2,128]{3,0,1,2:T(8,128)(2,1)S(1)} %copy-done.12), kind=kOutput, calls=%fused_computation.60 | convolution fusion | flops 279969792 | bytes 7602176 | tf_op jit(solution)/shard_map/ahd,chd->hac/dot_general | solution.py:32
  138.3 2.1 collective-permute-start.1
  140.4 2.2 select_convert_fusion.1
  145.2 1.7 fusion.46
  146.9 56.4 %collective-permute-done.1 = bf16[512,4,2,128]{3,0,1,2:T(8,128)(2,1)S(1)} collective-permute-done((bf16[512,4,2,128]{3,0,1,2:T(8,128)(2,1)S(1)}, bf16[512,4,2,128]{3,0,1,2:T(8,128)(2,1)S(1)}, u32[]{:S(2)}, u32[]{:S(2)}) %collective-permute-start.1) | collective-permute-done | bytes 1048608 | tf_op jit(solution)/shard_map/ppermute | solution.py:12
  203.6 32.4 %all-gather.5.cloned.1.call-done = bf16[2048,4,2,128]{3,0,1,2:T(8,128)(2,1)} async-done(((bf16[512,4,2,128]{3,0,1,2:T(8,128)(2,1)}), bf16[2048,4,2,128]{3,0,1,2:T(8,128)(2,1)}) %all-gather.5.cloned.1.call-update) | async-done | bytes 4194320 | tf_op jit(solution)/shard_map/all_gather | solution.py:153
  236.0 4.6 %copy.45 = bf16[4,512,4,2,128]{4,1,2,3,0:T(8,128)(2,1)} copy(bf16[4,512,4,2,128]{4,1,0,2,3:T(8,128)(2,1)} %bitcast.229) | data formatting | bytes 8388608 | tf_op jit(solution)/shard_map/while | solution.py:190
  240.6 40.9 %while.38 = (s32[]{:T(128)}, f32[512,4,128]{2,0,1:T(8,128)}, f32[512,4,2,128]{3,0,1,2:T(8,128)S(1)}, s32[3]{0:T(128)S(1)}, bf16[4,512,4,2,128]{4,1,2,3,0:T(8,128...) while((s32[]{:T(128)}, f32[512,4,128]{2,0,1:T(8,128)}, ...), condition=%wide.region_18.19_spmd, body=%wide.region_11.18_spmd.sunk | while | flops 1908146176 | bytes 45613352 | solution.py:190
  248.5 15.1 %conditional.8 = (f32[512,4,2,128]{3,0,1,2:T(8,128)S(1)}) conditional(s32[]{:T(128)} %convert_element_type.150, f32[512,4,2,128]{3,0,1,2:T(8,128)S(1)} %get-tuple-element.621, (bf16[4,512,4,2,128]{4,1,2,3,0:T(8,128)(2,1)}, s32[]{:T(128)}, bf16[512,4,2,128]{3,0,1,2:T(8,128)(2,1)}, f32[512,4,2,128]{3,0,1,2:T(8,128)S(1)}) %tuple.114), branch_computations={%region_16.16_spmd, %region_17.17_spmd} | conditional | flops 1091829760 | bytes 30408744 | solution.py:187
  249.9 3.7 %fusion.33 = f32[4,512,512]{2,1,0:T(8,128)} fusion(bf16[512,4,2,128]{3,0,1,2:T(8,128)(2,1)} %get-tuple-element.387, bf16[512,4,2,128]{3,0,1,2:T(8,128)(2,1)S(1)} %dynamic-slice_bitcast_fusion.2), kind=kOutput, calls=%fused_computation.49 | convolution fusion | flops 268435456 | bytes 5242880 | tf_op jit(solution)/shard_map/while/body/eval_jaxpr/cond/branch_1_fun/ahd,chd->hac/dot_general | solution.py:17
  253.6 5.7 %fusion.32 = f32[512,4,1,128]{3,0,1,2:T(8,128)} fusion(f32[4,512,512]{2,1,0:T(8,128)} %fusion.33, bf16[512,4,2,128]{3,0,1,2:T(8,128)(2,1)} %get-tuple-element.387, bf16[512,4,2,128]{3,0,1,2:T(8,128)(2,1)S(1)} %dynamic-slice_bitcast_fusion.2), kind=kOutput, calls=%fused_computation.45 | convolution fusion | flops 547618816 | bytes 6815744 | tf_op jit(solution)/shard_map/while/body/eval_jaxpr/cond/branch_1_fun/hac,ahd->chd/dot_general | solution.py:35
  259.3 3.8 %fusion.30 = f32[512,4,1,128]{3,0,1,2:T(8,128)S(1)} fusion(f32[4,512,512]{2,1,0:T(8,128)} %fusion.33, bf16[512,4,2,128]{3,0,1,2:T(8,128)(2,1)S(1)} %dynamic-slice_bitcast_fusion.2), kind=kOutput, calls=%fused_computation.43 | convolution fusion | flops 274726912 | bytes 5767168 | tf_op jit(solution)/shard_map/while/body/eval_jaxpr/cond/branch_1_fun/hac,ahd->chd/dot_general | solution.py:36
  266.3 15.1 %conditional.8 = (f32[512,4,2,128]{3,0,1,2:T(8,128)S(1)}) conditional(s32[]{:T(128)} %convert_element_type.150, f32[512,4,2,128]{3,0,1,2:T(8,128)S(1)} %get-tuple-element.621, (bf16[4,512,4,2,128]{4,1,2,3,0:T(8,128)(2,1)}, s32[]{:T(128)}, bf16[512,4,2,128]{3,0,1,2:T(8,128)(2,1)}, f32[512,4,2,128]{3,0,1,2:T(8,128)S(1)}) %tuple.114), branch_computations={%region_16.16_spmd, %region_17.17_spmd} | conditional | flops 1091829760 | bytes 30408744 | solution.py:187
  267.6 3.7 %fusion.33 = f32[4,512,512]{2,1,0:T(8,128)} fusion(bf16[512,4,2,128]{3,0,1,2:T(8,128)(2,1)} %get-tuple-element.387, bf16[512,4,2,128]{3,0,1,2:T(8,128)(2,1)S(1)} %dynamic-slice_bitcast_fusion.2), kind=kOutput, calls=%fused_computation.49 | convolution fusion | flops 268435456 | bytes 5242880 | tf_op jit(solution)/shard_map/while/body/eval_jaxpr/cond/branch_1_fun/ahd,chd->hac/dot_general | solution.py:17
  271.3 5.7 %fusion.32 = f32[512,4,1,128]{3,0,1,2:T(8,128)} fusion(f32[4,512,512]{2,1,0:T(8,128)} %fusion.33, bf16[512,4,2,128]{3,0,1,2:T(8,128)(2,1)} %get-tuple-element.387, bf16[512,4,2,128]{3,0,1,2:T(8,128)(2,1)S(1)} %dynamic-slice_bitcast_fusion.2), kind=kOutput, calls=%fused_computation.45 | convolution fusion | flops 547618816 | bytes 6815744 | tf_op jit(solution)/shard_map/while/body/eval_jaxpr/cond/branch_1_fun/hac,ahd->chd/dot_general | solution.py:35
  277.0 3.8 %fusion.30 = f32[512,4,1,128]{3,0,1,2:T(8,128)S(1)} fusion(f32[4,512,512]{2,1,0:T(8,128)} %fusion.33, bf16[512,4,2,128]{3,0,1,2:T(8,128)(2,1)S(1)} %dynamic-slice_bitcast_fusion.2), kind=kOutput, calls=%fused_computation.43 | convolution fusion | flops 274726912 | bytes 5767168 | tf_op jit(solution)/shard_map/while/body/eval_jaxpr/cond/branch_1_fun/hac,ahd->chd/dot_general | solution.py:36
  281.4 1.6 copy.70
  285.2 4.5 %maximum_bitcast_fusion = bf16[1,512,4,4,128]{4,3,2,1,0:T(4,128)(2,1)} fusion(bf16[512,4,2,128]{3,2,1,0:T(2,128)(2,1)S(1)} %copy.70, bf16[512,4,1,128]{3,2,1,0:T(2,128)(2,1)S(1)} %copy.48, bf16[512,4,1,128]{3,2,1,0:T(2,128)(2,1)S(1)} %copy-done.9), kind=kLoop, calls=%fused_computation.67 | loop fusion | flops 6291456 | bytes 4194304 | tf_op jit(solution)/shard_map/broadcast_in_dim | solution.py:196
  (98 shorter events, 28.5 us)
Async XLA Ops:
  7.2 7.8 %copy-start.17 = (s32[1,4,3]{1,0,2:T(1,128)S(1)}, s32[1,4,3]{1,0,2:T(1,128)}, u32[]{:S(2)}) copy-start(s32[1,4,3]{1,0,2:T(1,128)} %param.21) | copy-start | bytes 148
  7.2 9.5 %copy-start.16 = (f32[1,2048]{1,0:T(1,128)S(1)}, f32[1,2048]{1,0:T(1,128)}, u32[]{:S(2)}) copy-start(f32[1,2048]{1,0:T(1,128)} %param.18) | copy-start | bytes 24580
  7.2 10.2 %copy-start.15 = (s32[1,2048]{1,0:T(1,128)S(1)}, s32[1,2048]{1,0:T(1,128)}, u32[]{:S(2)}) copy-start(s32[1,2048]{1,0:T(1,128)} %param.19) | copy-start | bytes 24580
  7.2 11.0 %copy-start.18 = (s32[1,2048]{1,0:T(1,128)S(1)}, s32[1,2048]{1,0:T(1,128)}, u32[]{:S(2)}) copy-start(s32[1,2048]{1,0:T(1,128)} %param.20) | copy-start | bytes 24580
  7.2 98.6 %all-gather.3.cloned.1.call-start = ((), (), s32[]{:S(2)}) async-start(), calls=%async_computation | async-start | bytes 5242880 | tf_op jit(solution)/shard_map/all_gather | solution.py:86
  9.4 60.7 %copy-start.1 = (bf16[1,512,4,4,128]{4,1,2,3,0:T(8,128)(2,1)}, bf16[1,512,4,4,128]{4,1,2,3,0:T(8,128)(2,1)S(1)}, u32[]{:S(2)}) copy-start(bf16[1,512,4,4,128]{4,1,2,3,0:T(8,128)(2,1)S(1)} %copy.71) | copy-start | bytes 6291460
  10.6 225.4 %all-gather.5.cloned.1.call-start = ((), (), s32[]{:S(2)}) async-start(), calls=%async_computation.1 | async-start | bytes 5242880 | tf_op jit(solution)/shard_map/all_gather | solution.py:153
  10.6 59.5 %collective-permute-start = (bf16[512,4,2,128]{3,0,1,2:T(8,128)(2,1)}, bf16[512,4,2,128]{3,0,1,2:T(8,128)(2,1)S(1)}, u32[]{:S(2)}, u32[]{:S(2)}) collective-permute-start(bf16[512,4,2,128]{3,0,1,2:T(8,128)(2,1)} %slice.88), channel_id=1, source_target_pairs={{0,4},{4,8},{8,12},{1,5},{5,9},{9,13},{2,6},{6,10},{10,14},{3,7},{... | collective-permute-start | bytes 3145736 | tf_op jit(solution)/shard_map/ppermute | solution.py:12
  18.6 51.5 %copy-start.13 = (pred[512,512]{1,0:T(8,128)(4,1)}, pred[512,512]{1,0:T(8,128)(4,1)S(1)}, u32[]{:S(2)}) copy-start(pred[512,512]{1,0:T(8,128)(4,1)S(1)} %get-tuple-element.483) | copy-start | bytes 786436
  22.2 51.5 %copy-start.5 = (bf16[4,512,512]{2,1,0:T(8,128)(2,1)}, bf16[4,512,512]{2,1,0:T(8,128)(2,1)S(1)}, u32[]{:S(2)}) copy-start(bf16[4,512,512]{2,1,0:T(8,128)(2,1)S(1)} %get-tuple-element.485) | copy-start | bytes 6291460
  70.1 3.6 %copy-start.11 = (bf16[512,4,2,128]{3,0,1,2:T(8,128)(2,1)}, bf16[512,4,2,128]{3,0,1,2:T(8,128)(2,1)S(1)}, u32[]{:S(2)}) copy-start(bf16[512,4,2,128]{3,0,1,2:T(8,128)(2,1)S(1)} %collective-permute-done) | copy-start | bytes 3145732
  73.7 1.3 copy-start.7
  115.8 4.2 %copy-start.2 = (bf16[1,512,4,4,128]{4,1,2,3,0:T(8,128)(2,1)S(1)}, bf16[1,512,4,4,128]{4,1,2,3,0:T(8,128)(2,1)}, u32[]{:S(2)}) copy-start(bf16[1,512,4,4,128]{4,1,2,3,0:T(8,128)(2,1)} %copy-done.1) | copy-start | bytes 6291460
  122.9 0.8 copy-start.3
  122.9 7.8 %copy-start.10 = (bf16[512,4,1,128]{3,0,1,2:T(8,128)(2,1)S(1)}, bf16[512,4,1,128]{3,0,1,2:T(8,128)(2,1)}, u32[]{:S(2)}) copy-start(bf16[512,4,1,128]{3,0,1,2:T(8,128)(2,1)} %get-tuple-element.480) | copy-start | bytes 1572868
  125.9 6.6 %copy-start.4 = (bf16[512,4,128]{2,0,1:T(8,128)(2,1)S(1)}, bf16[512,4,128]{2,0,1:T(8,128)(2,1)}, u32[]{:S(2)}) copy-start(bf16[512,4,128]{2,0,1:T(8,128)(2,1)} %copy-done.3) | copy-start | bytes 1572868
  126.0 6.5 %copy-start.8 = (bf16[4,512,512]{2,1,0:T(8,128)(2,1)S(1)}, bf16[4,512,512]{2,1,0:T(8,128)(2,1)}, u32[]{:S(2)}) copy-start(bf16[4,512,512]{2,1,0:T(8,128)(2,1)} %copy-done.7) | copy-start | bytes 6291460
  126.0 7.4 %copy-start.12 = (bf16[512,4,2,128]{3,0,1,2:T(8,128)(2,1)S(1)}, bf16[512,4,2,128]{3,0,1,2:T(8,128)(2,1)}, u32[]{:S(2)}) copy-start(bf16[512,4,2,128]{3,0,1,2:T(8,128)(2,1)} %copy-done.11) | copy-start | bytes 3145732
  126.0 7.4 %copy-start.14 = (pred[512,512]{1,0:T(8,128)(4,1)S(1)}, pred[512,512]{1,0:T(8,128)(4,1)}, u32[]{:S(2)}) copy-start(pred[512,512]{1,0:T(8,128)(4,1)} %copy-done.13) | copy-start | bytes 786436
  137.3 3.1 %copy-start.19 = (f32[4,512,512]{2,1,0:T(8,128)S(1)}, f32[4,512,512]{2,1,0:T(8,128)}, u32[]{:S(2)}) copy-start(f32[4,512,512]{2,1,0:T(8,128)} %get-tuple-element.486) | copy-start | bytes 12582916
  138.3 65.0 %collective-permute-start.1 = (bf16[512,4,2,128]{3,0,1,2:T(8,128)(2,1)S(1)}, bf16[512,4,2,128]{3,0,1,2:T(8,128)(2,1)S(1)}, u32[]{:S(2)}, u32[]{:S(2)}) collective-permute-start(bf16[512,4,2,128]{3,0,1,2:T(8,128)(2,1)S(1)} %pad_maximum_fusion), channel_id=1, source_target_pairs={{4,0},{8,4},{12,8},{5,1},{9,5},{13,9},{6,2},{10,6},{14,10},{7,3},{... | collective-permute-start | bytes 3145736 | tf_op jit(solution)/shard_map/ppermute | solution.py:12
  140.4 2.3 copy-start.6
  259.3 3.8 %copy-start = (f32[512,4,1,128]{3,0,1,2:T(8,128)S(1)}, f32[512,4,1,128]{3,0,1,2:T(8,128)}, u32[]{:S(2)}) copy-start(f32[512,4,1,128]{3,0,1,2:T(8,128)} %fusion.32) | copy-start | bytes 3145732 | tf_op jit(solution)/shard_map/while/body/eval_jaxpr/cond
  277.0 3.8 %copy-start = (f32[512,4,1,128]{3,0,1,2:T(8,128)S(1)}, f32[512,4,1,128]{3,0,1,2:T(8,128)}, u32[]{:S(2)}) copy-start(f32[512,4,1,128]{3,0,1,2:T(8,128)} %fusion.32) | copy-start | bytes 3145732 | tf_op jit(solution)/shard_map/while/body/eval_jaxpr/cond
  281.4 3.8 %copy-start.9 = (bf16[512,4,1,128]{3,2,1,0:T(2,128)(2,1)S(1)}, bf16[512,4,1,128]{3,2,1,0:T(2,128)(2,1)}, u32[]{:S(2)}) copy-start(bf16[512,4,1,128]{3,2,1,0:T(2,128)(2,1)} %copy.47) | copy-start | bytes 1572868
Sparse Core Ops, SparseCore 0:
  10.7 95.0 all-gather.2
  126.0 109.8 all-gather.4
where the time goes:
time: 297 us
  waiting for transfers between devices  166 us (56%)
  matrix products  47.1 us (16%)
  local copies, waits for them, and re-layouts  27.4 us (9%)
  other arithmetic  27.3 us (9%)
  between operations  15 us (5%)
  loops' own time  8.06 us (3%)
  starting transfers between devices  5.62 us (2%)
    ppermute x2, waiting for transfers between devices, shifted_2(): return lax.ppermute(block, axis, route)  104 us
    all_gather x1, waiting for transfers between devices, shards(): lax.all_gather(pulled, 'ctx', axis=0, tiled=True)  32.4 us
    all_gather x1, waiting for transfers between devices, shards(): lax.all_gather(pairs, 'ctx', axis=0, tiled=True)  30 us
    dot_general x4, matrix products, pair_scores(): jnp.einsum('ahd,chd->hac', queries, keys, preferred_element_type=jnp.floa...  14.6 us
    dot_general x4, matrix products, attend_back(): jnp.einsum('hac,ahd->chd', edges, queries, preferred_element_type=jnp.flo...  13.3 us
    dot_general x4, matrix products, attend_back(): jnp.einsum('hac,ahd->chd', probs, grad_rows, preferred_element_type=jnp.f...  9.46 us
    while x3, local copies, waits for them, and re-layouts, shards(): lax.fori_loop(0, piece_pairs.shape[0], visit, (tuple(grad_q), tuple(grad_...  8.68 us
    unnamed x41, local copies, waits for them, and re-layouts  6.66 us
  transfers between devices with their start and end apart: 4, of which 4 were waited for; matrix products, arithmetic and copies ran while one was open for 11% of the time, Pallas kernels for 0%

commit v1 on v0

--- a/solution.py
+++ b/solution.py
@@ -4,6 +4,16 @@
 from jax.sharding import PartitionSpec as P
 
 BLOCK = 512
+
+
+def collect(x, axis, dim):
+    ways, here, lap = (lax.axis_size(axis), lax.axis_index(axis), x.shape[dim])
+    lengths = [n * ways if d == dim else n for d, n in enumerate(x.shape)]
+    full = lax.dynamic_update_slice_in_dim(jnp.zeros(lengths, x.dtype), x, here * lap, axis=dim)
+    for far in range(1, ways):
+        x = lax.ppermute(x, axis, [(d, (d + 1) % ways) for d in range(ways)])
+        full = lax.dynamic_update_slice_in_dim(full, x, (here - far) % ways * lap, axis=dim)
+    return full
 
 
 def shifted_2(block, axis, distance):
@@ -150,9 +160,7 @@
     piece_pairs = lax.all_gather(pairs, "ctx", axis=0, tiled=True).reshape(
         -1, block, heads, 2, width
     )
-    piece_pulled = lax.all_gather(pulled, "ctx", axis=0, tiled=True).reshape(
-        -1, block, heads, 2, width
-    )
+    piece_pulled = collect(pulled, "ctx", 0).reshape(-1, block, heads, 2, width)
 
     def visit(index, acc):
         sums, owned = acc

time: 297 us -> 288 us (0.970)
  waiting for transfers between devices: 166 us -> 153 us
  starting transfers between devices: 5.62 us -> 15.2 us
  matrix products: 47.1 us -> 43.4 us
    ppermute x0 -> x3, waiting for transfers between devices: none -> 77.2 us  [collect(): x = lax.ppermute(x, axis, [(d, (d + 1) % ways) for d in range(ways)])]
    ppermute x2, waiting for transfers between devices: 104 us -> 48 us  [shifted_2(): return lax.ppermute(block, axis, route)]
    all_gather x1 -> x0, waiting for transfers between devices: 32.4 us -> none  [shards(): lax.all_gather(pulled, 'ctx', axis=0, tiled=True)]
    ppermute x0 -> x3, starting transfers between devices: none -> 9.8 us  [collect(): x = lax.ppermute(x, axis, [(d, (d + 1) % ways) for d in range(ways)])]
    cond x4, local copies, waits for them, and re-layouts: 0.01 us -> 3.9 us
    while x3, local copies, waits for them, and re-layouts: 8.68 us -> 5.08 us  [shards(): lax.fori_loop(0, piece_pairs.shape[0], visit, (tuple(grad_q), tuple(grad_...]
    unnamed x41 -> x37, local copies, waits for them, and re-layouts: 6.66 us -> 4.8 us
  transfers between devices with their start and end apart: 4 -> 6, of which waited for: 4 -> 5; matrix products, arithmetic and copies ran while one was open for 11% -> 9% of each run, Pallas kernels for 0% -> 0%
where the time goes in v1:
time: 288 us; the launch traced here: 287 us
  waiting for transfers between devices  153 us (53%)
  matrix products  43.4 us (15%)
  other arithmetic  26.9 us (9%)
  local copies, waits for them, and re-layouts  25.9 us (9%)
  starting transfers between devices  15.2 us (5%)
  between operations  15.2 us (5%)
  loops' own time  7.24 us (3%)
    ppermute x3, waiting for transfers between devices, collect(): x = lax.ppermute(x, axis, [(d, (d + 1) % ways) for d in range(ways)])  77.2 us
    ppermute x2, waiting for transfers between devices, shifted_2(): return lax.ppermute(block, axis, route)  48 us
    all_gather x1, waiting for transfers between devices, shards(): lax.all_gather(pairs, 'ctx', axis=0, tiled=True)  28 us
    dot_general x4, matrix products, attend_back(): jnp.einsum('hac,ahd->chd', edges, queries, preferred_element_type=jnp.flo...  13.2 us
    dot_general x4, matrix products, pair_scores(): jnp.einsum('ahd,chd->hac', queries, keys, preferred_element_type=jnp.floa...  11.7 us
    ppermute x3, starting transfers between devices, collect(): x = lax.ppermute(x, axis, [(d, (d + 1) % ways) for d in range(ways)])  9.8 us
    dot_general x4, matrix products, attend_back(): jnp.einsum('hac,ahd->chd', probs, grad_rows, preferred_element_type=jnp.f...  6.95 us
  transfers between devices with their start and end apart: 6, of which 5 were waited for; matrix products, arithmetic and copies ran while one was open for 9% of the time, Pallas kernels for 0%

profile of v1, /device:TPU:12, one launch (start us, length us, event | category | flops | bytes accessed | tf_op | source)
XLA Modules:
  0.0 287.2 jit_solution(12508565973019763576)
XLA Ops:
  7.2 2.1 copy.78
  10.6 3.5 %collective-permute-start = (bf16[512,4,2,128]{3,0,1,2:T(8,128)(2,1)}, bf16[512,4,2,128]{3,0,1,2:T(8,128)(2,1)}, u32[]{:S(2)}, u32[]{:S(2)}) collective-permute-start(bf16[512,4,2,128]{3,0,1,2:T(8,128)(2,1)} %slice.88), channel_id=1, source_target_pairs={{0,4},{4,8},{8,12},{1,5},{5,9},{9,13},{2,6},{6,10},{10,14},{3,7},{... | collective-permute-start | bytes 3145736 | tf_op jit(solution)/shard_map/ppermute | solution.py:22
  17.7 3.6 %select_convert_fusion.3 = (bf16[4,512,512]{2,1,0:T(8,128)(2,1)S(1)}, f32[4,512,512]{2,1,0:T(8,128)}) fusion(pred[512,512]{1,0:T(8,128)(4,1)S(1)} %get-tuple-element.484, bf16[512,4,4,128]{3,0,1,2:T(8,128)(2,1)S(1)} %bitcast.218), kind=kOutput, calls=%fused_computation.64 | convolution fusion | flops 275775488 | bytes 7602176 | tf_op jit(solution)/shard_map/ahd,chd->hac/dot_general | solution.py:27
  22.0 48.0 %collective-permute-done = bf16[512,4,2,128]{3,0,1,2:T(8,128)(2,1)} collective-permute-done((bf16[512,4,2,128]{3,0,1,2:T(8,128)(2,1)}, bf16[512,4,2,128]{3,0,1,2:T(8,128)(2,1)}, u32[]{:S(2)}, u32[]{:S(2)}) %collective-permute-start) | collective-permute-done | bytes 1048608 | tf_op jit(solution)/shard_map/ppermute | solution.py:22
  70.0 4.6 %select_convert_fusion.2 = (bf16[4,512,512]{2,1,0:T(8,128)(2,1)S(1)}, f32[4,512,512]{2,1,0:T(8,128)}) fusion(pred[512,512]{1,0:T(8,128)(4,1)S(1)} %get-tuple-element.483, bf16[512,4,2,128]{3,0,1,2:T(8,128)(2,1)} %collective-permute-done, bf16[512,4,4,128]{3,0,1,2:T(8,128)(2,1)S(1)} %bitcast.220), kind=kOutput, calls=%fused_computation.62 | convolution fusion | flops 275775488 | bytes 7602176 | tf_op jit(solution)/shard_map/ahd,chd->hac/dot_general | solution.py:27
  77.7 28.0 %all-gather.2.cloned.1.call-done = bf16[2048,4,2,128]{3,0,1,2:T(8,128)(2,1)} async-done(((bf16[512,4,2,128]{3,0,1,2:T(8,128)(2,1)}), bf16[2048,4,2,128]{3,0,1,2:T(8,128)(2,1)}) %all-gather.2.cloned.1.call-update) | async-done | bytes 4194320 | tf_op jit(solution)/shard_map/all_gather | solution.py:96
  105.7 4.6 %copy.33 = bf16[4,512,4,2,128]{4,1,2,3,0:T(8,128)(2,1)} copy(bf16[4,512,4,2,128]{4,1,0,2,3:T(8,128)(2,1)} %bitcast.230) | data formatting | bytes 8388608 | tf_op jit(solution)/shard_map/while | solution.py:115
  110.3 4.8 %while.37 = (s32[]{:T(128)}, f32[512,4,128]{2,0,1:T(8,128)S(1)}, s32[3]{0:T(128)S(1)}, bf16[4,512,4,2,128]{4,1,2,3,0:T(8,128)(2,1)}, bf16[512,4,1,128]{3,0,1,2:T(8,128)(2,1)S(1)}, /*index=5*/s32[]{:T(128)}) while((s32[]{:T(128)}, f32[512,4,128]{2,0,1:T(8,128)S(1)}, s32[3]{0:T(128)S(1)}, bf16[4,512,4,2,128]{4,1,2,3,0:T(8,128)(2,1)}, ...), condition=%wide.region_5.6_spmd, body=%wide.region_1.5_spmd.sunk | while | flops 543424512 | bytes 5767345 | solution.py:115
  116.2 2.5 fusion.59
  118.7 3.0 %multiply_convert_fusion.5 = (bf16[512,4,128]{2,0,1:T(8,128)(2,1)S(1)}, bf16[1,512,4,128]{3,1,2,0:T(8,128)(2,1)S(1)}) fusion(f32[512,4,128]{2,0,1:T(8,128)S(1)} %get-tuple-element.405, f32[512,4]{0,1:T(4,128)S(1)} %get-tuple-element.489, f32[512,4]{0,1:T(4,128)S(1)} %get-tuple-element.490, f32[512]{0:T(512)S(1)} %fusion.71, f32[512,4]{0,1:T(4,128)S(1)} %add_rsqrt_fusion, ...), kind=kLoop, calls=%fused_computation.95 | loop fusion | flops 3407872 | bytes 3180544 | tf_op jit(solution)/shard_map/convert_element_type | solution.py:138
  122.6 3.3 %select_convert_fusion = bf16[4,512,512]{2,1,0:T(8,128)(2,1)S(1)} fusion(f32[4,512,512]{2,1,0:T(8,128)S(1)} %copy-done.17, bf16[512,4,128]{2,0,1:T(8,128)(2,1)S(1)} %get-tuple-element.478, pred[512,512]{1,0:T(8,128)(4,1)S(1)} %copy-done.11, bf16[512,4,2,128]{3,0,1,2:T(8,128)(2,1)} %collective-permute-done), kind=kOutput, calls=%fused_computation.60 | convolution fusion | flops 279969792 | bytes 7602176 | tf_op jit(solution)/shard_map/ahd,chd->hac/dot_general | solution.py:42
  127.0 2.4 collective-permute-start.2
  129.5 1.9 collective-permute-start.1
  131.4 2.2 select_convert_fusion.1
  133.6 18.5 %collective-permute-done.2 = bf16[512,4,2,128]{3,0,1,2:T(8,128)(2,1)S(1)} collective-permute-done((bf16[512,4,2,128]{3,0,1,2:T(8,128)(2,1)S(1)}, bf16[512,4,2,128]{3,0,1,2:T(8,128)(2,1)S(1)}, u32[]{:S(2)}, u32[]{:S(2)}) %collective-permute-start.2) | collective-permute-done | bytes 1048608 | tf_op jit(solution)/shard_map/ppermute | solution.py:14
  152.2 7.4 %collective-permute-start.3 = (bf16[512,4,2,128]{3,0,1,2:T(8,128)(2,1)S(1)}, bf16[512,4,2,128]{3,0,1,2:T(8,128)(2,1)S(1)}, u32[]{:S(2)}, u32[]{:S(2)}) collective-permute-start(bf16[512,4,2,128]{3,0,1,2:T(8,128)(2,1)S(1)} %collective-permute-done.2), channel_id=1, source_target_pairs={{0,4},{4,8},{8,12},{12,0},{1,5},{5,9},{9,13},{13,1},{2,6},{6,10},{... | collective-permute-start | bytes 3145736 | tf_op jit(solution)/shard_map/ppermute | solution.py:14
  166.1 2.9 fusion.46
  169.0 15.2 %collective-permute-done.3 = bf16[512,4,2,128]{3,0,1,2:T(8,128)(2,1)S(1)} collective-permute-done((bf16[512,4,2,128]{3,0,1,2:T(8,128)(2,1)S(1)}, bf16[512,4,2,128]{3,0,1,2:T(8,128)(2,1)S(1)}, u32[]{:S(2)}, u32[]{:S(2)}) %collective-permute-start.3) | collective-permute-done | bytes 1048608 | tf_op jit(solution)/shard_map/ppermute | solution.py:14
  185.7 43.5 %collective-permute-done.4 = bf16[512,4,2,128]{3,0,1,2:T(8,128)(2,1)S(1)} collective-permute-done((bf16[512,4,2,128]{3,0,1,2:T(8,128)(2,1)S(1)}, bf16[512,4,2,128]{3,0,1,2:T(8,128)(2,1)S(1)}, u32[]{:S(2)}, u32[]{:S(2)}) %collective-permute-start.4) | collective-permute-done | bytes 1048608 | tf_op jit(solution)/shard_map/ppermute | solution.py:14
  229.3 2.3 copy.48
  231.6 40.5 %while.38 = (s32[]{:T(128)}, f32[512,4,128]{2,0,1:T(8,128)}, f32[512,4,2,128]{3,0,1,2:T(8,128)S(1)}, s32[3]{0:T(128)S(1)}, bf16[4,512,4,2,128]{4,1,2,3,0:T(8,128...) while((s32[]{:T(128)}, f32[512,4,128]{2,0,1:T(8,128)}, ...), condition=%wide.region_18.19_spmd, body=%wide.region_11.18_spmd.sunk | while | flops 1908146176 | bytes 58196264 | solution.py:198
  239.0 15.3 %conditional.8 = (f32[512,4,2,128]{3,0,1,2:T(8,128)S(1)}) conditional(s32[]{:T(128)} %convert_element_type.150, f32[512,4,2,128]{3,0,1,2:T(8,128)S(1)} %get-tuple-element.621, (bf16[4,512,4,2,128]{4,1,2,3,0:T(8,128)(2,1)}, s32[]{:T(128)}, bf16[512,4,2,128]{3,0,1,2:T(8,128)(2,1)}, f32[512,4,2,128]{3,0,1,2:T(8,128)S(1)}) %tuple.114), branch_computations={%region_16.16_spmd, %region_17.17_spmd} | conditional | flops 1091829760 | bytes 42991656 | solution.py:195
  242.1 1.9 copy-done
  244.0 2.6 fusion.30
  246.6 5.7 %fusion.32 = f32[512,4,1,128]{3,0,1,2:T(8,128)} fusion(f32[4,512,512]{2,1,0:T(8,128)} %copy-done, bf16[512,4,2,128]{3,0,1,2:T(8,128)(2,1)} %get-tuple-element.387, bf16[512,4,2,128]{3,0,1,2:T(8,128)(2,1)S(1)} %dynamic-slice_bitcast_fusion.2), kind=kOutput, calls=%fused_computation.45 | convolution fusion | flops 547618816 | bytes 6815744 | tf_op jit(solution)/shard_map/while/body/eval_jaxpr/cond/branch_1_fun/hac,ahd->chd/dot_general | solution.py:45
  252.3 2.0 maximum_add_fusion
  256.8 15.3 %conditional.8 = (f32[512,4,2,128]{3,0,1,2:T(8,128)S(1)}) conditional(s32[]{:T(128)} %convert_element_type.150, f32[512,4,2,128]{3,0,1,2:T(8,128)S(1)} %get-tuple-element.621, (bf16[4,512,4,2,128]{4,1,2,3,0:T(8,128)(2,1)}, s32[]{:T(128)}, bf16[512,4,2,128]{3,0,1,2:T(8,128)(2,1)}, f32[512,4,2,128]{3,0,1,2:T(8,128)S(1)}) %tuple.114), branch_computations={%region_16.16_spmd, %region_17.17_spmd} | conditional | flops 1091829760 | bytes 42991656 | solution.py:195
  259.9 1.9 copy-done
  261.8 2.6 fusion.30
  264.4 5.7 %fusion.32 = f32[512,4,1,128]{3,0,1,2:T(8,128)} fusion(f32[4,512,512]{2,1,0:T(8,128)} %copy-done, bf16[512,4,2,128]{3,0,1,2:T(8,128)(2,1)} %get-tuple-element.387, bf16[512,4,2,128]{3,0,1,2:T(8,128)(2,1)S(1)} %dynamic-slice_bitcast_fusion.2), kind=kOutput, calls=%fused_computation.45 | convolution fusion | flops 547618816 | bytes 6815744 | tf_op jit(solution)/shard_map/while/body/eval_jaxpr/cond/branch_1_fun/hac,ahd->chd/dot_general | solution.py:45
  270.0 2.0 maximum_add_fusion
  275.8 4.5 %maximum_bitcast_fusion = bf16[1,512,4,4,128]{4,3,2,1,0:T(4,128)(2,1)} fusion(bf16[512,4,2,128]{3,2,1,0:T(2,128)(2,1)S(1)} %copy.77, bf16[512,4,1,128]{3,2,1,0:T(2,128)(2,1)S(1)} %copy.51, bf16[512,4,1,128]{3,2,1,0:T(2,128)(2,1)S(1)} %copy-done.8), kind=kLoop, calls=%fused_computation.67 | loop fusion | flops 6291456 | bytes 4194304 | tf_op jit(solution)/shard_map/broadcast_in_dim | solution.py:204
  (102 shorter events, 36.5 us)
Async XLA Ops:
  7.2 7.0 %copy-start.14 = (s32[1,4,3]{1,0,2:T(1,128)S(1)}, s32[1,4,3]{1,0,2:T(1,128)}, u32[]{:S(2)}) copy-start(s32[1,4,3]{1,0,2:T(1,128)} %param.21) | copy-start | bytes 148
  7.2 8.6 %copy-start.13 = (f32[1,2048]{1,0:T(1,128)S(1)}, f32[1,2048]{1,0:T(1,128)}, u32[]{:S(2)}) copy-start(f32[1,2048]{1,0:T(1,128)} %param.18) | copy-start | bytes 24580
  7.2 9.3 %copy-start.12 = (s32[1,2048]{1,0:T(1,128)S(1)}, s32[1,2048]{1,0:T(1,128)}, u32[]{:S(2)}) copy-start(s32[1,2048]{1,0:T(1,128)} %param.19) | copy-start | bytes 24580
  7.2 10.1 %copy-start.15 = (s32[1,2048]{1,0:T(1,128)S(1)}, s32[1,2048]{1,0:T(1,128)}, u32[]{:S(2)}) copy-start(s32[1,2048]{1,0:T(1,128)} %param.20) | copy-start | bytes 24580
  7.2 98.5 %all-gather.2.cloned.1.call-start = ((), (), s32[]{:S(2)}) async-start(), calls=%async_computation | async-start | bytes 5242880 | tf_op jit(solution)/shard_map/all_gather | solution.py:96
  9.4 60.7 %copy-start.2 = (bf16[1,512,4,4,128]{4,1,2,3,0:T(8,128)(2,1)}, bf16[1,512,4,4,128]{4,1,2,3,0:T(8,128)(2,1)S(1)}, u32[]{:S(2)}) copy-start(bf16[1,512,4,4,128]{4,1,2,3,0:T(8,128)(2,1)S(1)} %copy.78) | copy-start | bytes 6291460
  10.6 59.5 %collective-permute-start = (bf16[512,4,2,128]{3,0,1,2:T(8,128)(2,1)}, bf16[512,4,2,128]{3,0,1,2:T(8,128)(2,1)}, u32[]{:S(2)}, u32[]{:S(2)}) collective-permute-start(bf16[512,4,2,128]{3,0,1,2:T(8,128)(2,1)} %slice.88), channel_id=1, source_target_pairs={{0,4},{4,8},{8,12},{1,5},{5,9},{9,13},{2,6},{6,10},{10,14},{3,7},{... | collective-permute-start | bytes 3145736 | tf_op jit(solution)/shard_map/ppermute | solution.py:22
  17.7 52.3 %copy-start.10 = (pred[512,512]{1,0:T(8,128)(4,1)}, pred[512,512]{1,0:T(8,128)(4,1)S(1)}, u32[]{:S(2)}) copy-start(pred[512,512]{1,0:T(8,128)(4,1)S(1)} %get-tuple-element.483) | copy-start | bytes 786436
  21.3 53.3 %copy-start.4 = (bf16[4,512,512]{2,1,0:T(8,128)(2,1)}, bf16[4,512,512]{2,1,0:T(8,128)(2,1)S(1)}, u32[]{:S(2)}) copy-start(bf16[4,512,512]{2,1,0:T(8,128)(2,1)S(1)} %get-tuple-element.485) | copy-start | bytes 6291460
  74.6 1.3 copy-start.6
  110.3 5.8 %copy-start.9 = (bf16[1,512,4,128]{3,2,1,0:T(4,128)(2,1)S(1)}, bf16[1,512,4,128]{3,2,1,0:T(4,128)(2,1)}, u32[]{:S(2)}) copy-start(bf16[1,512,4,128]{3,2,1,0:T(4,128)(2,1)} %param.17) | copy-start | bytes 1572868
  115.1 50.9 %copy-start.1 = (bf16[512,4,1,128]{3,0,1,2:T(8,128)(2,1)}, bf16[512,4,1,128]{3,0,1,2:T(8,128)(2,1)S(1)}, u32[]{:S(2)}) copy-start(bf16[512,4,1,128]{3,0,1,2:T(8,128)(2,1)S(1)} %get-tuple-element.648) | copy-start | bytes 1572868
  115.5 6.2 %copy-start.7 = (bf16[4,512,512]{2,1,0:T(8,128)(2,1)S(1)}, bf16[4,512,512]{2,1,0:T(8,128)(2,1)}, u32[]{:S(2)}) copy-start(bf16[4,512,512]{2,1,0:T(8,128)(2,1)} %copy-done.6) | copy-start | bytes 6291460
  116.1 6.4 %copy-start.11 = (pred[512,512]{1,0:T(8,128)(4,1)S(1)}, pred[512,512]{1,0:T(8,128)(4,1)}, u32[]{:S(2)}) copy-start(pred[512,512]{1,0:T(8,128)(4,1)} %copy-done.10) | copy-start | bytes 786436
  116.2 6.4 %copy-start.17 = (f32[4,512,512]{2,1,0:T(8,128)S(1)}, f32[4,512,512]{2,1,0:T(8,128)}, u32[]{:S(2)}) copy-start(f32[4,512,512]{2,1,0:T(8,128)} %get-tuple-element.488) | copy-start | bytes 12582916
  122.6 3.3 %copy-start.3 = (bf16[1,512,4,4,128]{4,1,2,3,0:T(8,128)(2,1)S(1)}, bf16[1,512,4,4,128]{4,1,2,3,0:T(8,128)(2,1)}, u32[]{:S(2)}) copy-start(bf16[1,512,4,4,128]{4,1,2,3,0:T(8,128)(2,1)} %copy-done.2) | copy-start | bytes 6291460
  125.9 5.4 %copy-start.16 = (f32[4,512,512]{2,1,0:T(8,128)S(1)}, f32[4,512,512]{2,1,0:T(8,128)}, u32[]{:S(2)}) copy-start(f32[4,512,512]{2,1,0:T(8,128)} %get-tuple-element.486) | copy-start | bytes 12582916
  127.0 25.2 %collective-permute-start.2 = (bf16[512,4,2,128]{3,0,1,2:T(8,128)(2,1)S(1)}, bf16[512,4,2,128]{3,0,1,2:T(8,128)(2,1)S(1)}, u32[]{:S(2)}, u32[]{:S(2)}) collective-permute-start(bf16[512,4,2,128]{3,0,1,2:T(8,128)(2,1)S(1)} %pad_maximum_fusion.1), channel_id=1, source_target_pairs={{0,4},{4,8},{8,12},{12,0},{1,5},{5,9},{9,13},{13,1},{2,6},{6,10},{... | collective-permute-start | bytes 3145736 | tf_op jit(solution)/shard_map/ppermute | solution.py:14
  129.5 55.8 %collective-permute-start.1 = (bf16[512,4,2,128]{3,0,1,2:T(8,128)(2,1)S(1)}, bf16[512,4,2,128]{3,0,1,2:T(8,128)(2,1)S(1)}, u32[]{:S(2)}, u32[]{:S(2)}) collective-permute-start(bf16[512,4,2,128]{3,0,1,2:T(8,128)(2,1)S(1)} %pad_maximum_fusion), channel_id=1, source_target_pairs={{4,0},{8,4},{12,8},{5,1},{9,5},{13,9},{6,2},{10,6},{14,10},{7,3},{... | collective-permute-start | bytes 3145736 | tf_op jit(solution)/shard_map/ppermute | solution.py:22
  152.2 32.0 %collective-permute-start.3 = (bf16[512,4,2,128]{3,0,1,2:T(8,128)(2,1)S(1)}, bf16[512,4,2,128]{3,0,1,2:T(8,128)(2,1)S(1)}, u32[]{:S(2)}, u32[]{:S(2)}) collective-permute-start(bf16[512,4,2,128]{3,0,1,2:T(8,128)(2,1)S(1)} %collective-permute-done.2), channel_id=1, source_target_pairs={{0,4},{4,8},{8,12},{12,0},{1,5},{5,9},{9,13},{13,1},{2,6},{6,10},{... | collective-permute-start | bytes 3145736 | tf_op jit(solution)/shard_map/ppermute | solution.py:14
  166.0 18.2 %copy-start.5 = (bf16[4,512,512]{2,1,0:T(8,128)(2,1)S(1)}, bf16[4,512,512]{2,1,0:T(8,128)(2,1)}, u32[]{:S(2)}) copy-start(bf16[4,512,512]{2,1,0:T(8,128)(2,1)} %copy-done.4) | copy-start | bytes 6291460
  184.2 44.9 %collective-permute-start.4 = (bf16[512,4,2,128]{3,0,1,2:T(8,128)(2,1)S(1)}, bf16[512,4,2,128]{3,0,1,2:T(8,128)(2,1)S(1)}, u32[]{:S(2)}, u32[]{:S(2)}) collective-permute-start(bf16[512,4,2,128]{3,0,1,2:T(8,128)(2,1)S(1)} %collective-permute-done.3), channel_id=1, source_target_pairs={{0,4},{4,8},{8,12},{12,0},{1,5},{5,9},{9,13},{13,1},{2,6},{6,10},{... | collective-permute-start | bytes 3145736 | tf_op jit(solution)/shard_map/ppermute | solution.py:14
  242.1 2.0 copy-start
  259.8 2.0 copy-start
  272.1 3.8 %copy-start.8 = (bf16[512,4,1,128]{3,2,1,0:T(2,128)(2,1)S(1)}, bf16[512,4,1,128]{3,2,1,0:T(2,128)(2,1)}, u32[]{:S(2)}) copy-start(bf16[512,4,1,128]{3,2,1,0:T(2,128)(2,1)} %copy.50) | copy-start | bytes 1572868
Sparse Core Ops, SparseCore 0:
  10.7 94.9 all-gather.1
